TPU v7x, 256 devices: a whole 4x4x8 slice. The times are simulated.
256 devices in a mesh: ka: 64 (over x, y, z_hi, core), ot: 4 (over z_lo).
Axes of the slice: x: 4, y: 4, z: 8 (z_hi: 2, z_lo: 4; z = z_hi * 4 + z_lo), core: 2. Of those that a mesh axis runs over, the one named last changes fastest.
Arguments:
- green_coeff: bfloat16 [2304, 128, 128], P('ka', 'ot'), may hold values from -6 to 6
- screened: bfloat16 [2304, 256, 256], P(None, ('ot', 'ka')), may hold values from -6 to 6
- band_energy: float32 [2304, 2], P('ka'), may hold values from -4 to 4
- time_basis: float32 [64, 128], replicated, may hold values from -0.75 to 0.75
- projector: float32 [128, 64], replicated, may hold values from -0.5 to 0.5
- memory_kernel: float32 [64, 64], replicated, may hold values from -0.09375 to 0.09375
Outputs:
- sigma_coeff: bfloat16 [2304, 128, 128], P('ka', 'ot')
- green_next: bfloat16 [2304, 128, 128], P('ka', 'ot')
All inputs are finite; a program needn't handle non-finite values.
Results may differ from a plain program's by a relative error of at most 0.013.
Values may be sent and summed in bfloat16 or wider, within the bound.
A program may use at most 64 MiB of HBM per device.

v0:
```python
import functools
import math

import jax
import jax.numpy as jnp
import numpy as np
from jax import lax
from jax.experimental import pallas as pl
from jax.experimental.pallas import tpu as pltpu
from jax.sharding import PartitionSpec as P

STEP_SIZE = 0.25
MESH = pl.DeviceIdType.MESH
BF = jnp.bfloat16
F32 = jnp.float32
PAD = 24


def phase_tables(lattice, block, group):
    kx_rows = group * block // lattice
    half = block // 2
    cosine = lambda a, b: np.cos(2.0 * math.pi * (a * b % lattice) / lattice)
    sine = lambda a, b: np.sin(2.0 * math.pi * (a * b % lattice) / lattice)
    idx = np.arange(lattice)
    cx, sx = cosine(idx[:, None], idx[None, :]), sine(idx[:, None], idx[None, :])
    x_fwd = np.concatenate([cx, sx], axis=1)
    x_inv = np.concatenate([cx, -sx], axis=1)
    row = np.arange(group * 2 * PAD)
    place, inner = row // PAD, row % PAD
    kk = (place // 2) * block + (place % 2) * half + inner
    valid = inner < half
    kx_of, ky_of = kk // lattice, kk % lattice
    lat_row = np.arange(kx_rows * lattice)
    rx_of, ry_of = lat_row // lattice, lat_row % lattice
    same = (rx_of[:, None] == kx_of[None, :]) & valid[None, :]
    cy = np.where(same, cosine(ry_of[:, None], ky_of[None, :]), 0.0)
    sy = np.where(same, sine(ry_of[:, None], ky_of[None, :]), 0.0)
    y_fwd = np.concatenate([cy, sy], axis=1)
    y_inv = np.concatenate([cy.T, -sy.T], axis=1)
    return [t.astype(np.float32) for t in (x_fwd, x_inv, y_fwd, y_inv)]


def split(value):
    high = value.astype(BF)
    return high, (value - high.astype(F32)).astype(BF)


def dot(left, right):
    return jnp.dot(left, right, preferred_element_type=F32)


def kernel(
    green_ref, screen_ref, energy_ref, basis_ref, proj_ref, memk_ref,
    xf_ref, xi_ref, yf_ref, yi_ref,
    sigma_ref, next_ref,
    w_raw, wre_full, wim_full, pages, packed1, landed1, packed2, landed2, ytab, utab, xbuf,
    tb, pb, pq, kb, pt, partner, gmat, amat, skm,
    wsem, lsem, ssem1, rsem1, ssem2, rsem2, psem, qsem,
):
    ka, ot = lax.axis_index("ka"), lax.axis_index("ot")
    half, orbital = ot % 2, ot // 2
    mine, place = ka // 4, half * 4 + ka % 4
    count_k, rows_m, width = green_ref.shape
    hk = count_k // 2

    def device_of(grp, slot):
        return (grp * 4 + slot % 4, orbital * 2 + slot // 4)

    barrier = pltpu.get_barrier_semaphore()

    def greet(step, carry):
        slot = (place + step) % 8
        grp = (mine + step // 8) % 16
        pl.semaphore_signal(barrier, inc=1, device_id=device_of(grp, slot), device_id_type=MESH)
        return carry

    lax.fori_loop(1, 128, greet, 0)
    w_copy = pltpu.make_async_copy(screen_ref, w_raw, wsem)
    w_copy.start()

    lane64 = lax.broadcasted_iota(jnp.int32, (1, width), 1)
    low64 = lane64 < 64
    low32 = lane64 % 64 < 32
    minus_low = jnp.where(low64, -1.0, 1.0).astype(F32)

    def times_i(value):
        return pltpu.roll(value, 64, 1) * minus_low

    basis_t = basis_ref[...].T
    t_high, t_low = split(basis_t)
    t_cat = jnp.concatenate([t_high, t_low], axis=1)

    def rows_step(r, carry):
        parts = []
        both = [green_ref[r].astype(F32), green_ref[hk + r].astype(F32)]
        turned = [pltpu.roll(v, 64, 1) for v in both]
        for v, u in zip(both, turned):
            parts.append(jnp.where(low64, v, u))
        for v, u in zip(both, turned):
            parts.append(jnp.where(low64, u, v))
        right = jnp.concatenate(parts, axis=0).astype(BF)
        out = lax.dot_general(
            t_cat, right, (((1,), (1,)), ((), ())), preferred_element_type=F32
        )
        pages[pl.ds(r, 128, stride=PAD), :] = out
        return carry

    for r in range(hk):
        rows_step(r, 0)

    pl.semaphore_wait(barrier, 127)

    def send1(t, carry):
        grp = (mine + t) % 16
        for slot in range(8):
            q = (slot // 4) * 64 + grp * 4 + slot % 4
            start = pl.multiple_of(q * PAD, 8)
            value = pages[pl.ds(start, hk), :].astype(BF)
            packed1[grp, slot] = value.reshape(hk // 2, 2, width)
        for slot in range(8):
            @pl.when((t != 0) | (slot != place))
            def _():
                pltpu.make_async_remote_copy(
                    src_ref=packed1.at[grp, slot], dst_ref=landed1.at[mine, place],
                    send_sem=ssem1, recv_sem=rsem1.at[t],
                    device_id=device_of(grp, slot), device_id_type=MESH,
                ).start()
        return carry

    lax.fori_loop(0, 16, send1, 0)
    own1 = pltpu.make_async_copy(packed1.at[mine, place], landed1.at[mine, place], lsem)
    own1.start()

    zeros = jnp.zeros((64, 128), F32)
    basis = basis_ref[...]
    wide = jnp.concatenate(
        [jnp.concatenate([basis, zeros], axis=1), jnp.concatenate([zeros, basis], axis=1)], axis=0
    )
    high, low = split(wide)
    tb[0:128, :] = high
    tb[128:256, :] = low
    proj = proj_ref[...].T
    blank = jnp.zeros((128, 64), F32)
    left, right = jnp.concatenate([proj, blank], axis=1), jnp.concatenate([blank, proj], axis=1)
    for offset, piece in ((0, left), (128, right)):
        high, low = split(piece)
        pb[offset:offset + 128, :] = high
        pb[256 + offset:256 + offset + 128, :] = low
    pt[0:128, :] = left
    for grp in range(16):
        for h in range(2):
            pt[pl.ds(128 + grp * 8 + h * 4, 4), :] = pt[pl.ds(h * 64 + grp * 4, 4), :]
    left = pt[128:256, :]
    right = pltpu.roll(left, 64, 1)
    for offset, piece in ((0, left), (128, right)):
        high, low = split(piece)
        pq[offset:offset + 128, :] = high
        pq[256 + offset:256 + offset + 128, :] = low
    memk = memk_ref[...]
    blank = jnp.zeros((64, 64), F32)
    wide = jnp.concatenate(
        [jnp.concatenate([memk, blank], axis=1), jnp.concatenate([blank, memk], axis=1)], axis=0
    )
    high, low = split(wide)
    kb[0:128, :] = high
    kb[128:256, :] = low
    w_copy.wait()
    scale = 1.0 / w_raw.shape[0]

    def widen(i, carry):
        at = pl.ds(pl.multiple_of(i * 96, 32), 96)
        value = w_raw[at, :].astype(F32) * scale
        wre_full[at, :] = value[:, :128]
        wim_full[at, :] = value[:, 128:]
        return carry

    lax.fori_loop(0, 24, widen, 0)
    xbuf[...] = jnp.zeros_like(xbuf)
    own1.wait()

    def arrive1(t, carry):
        grp = (mine + 16 - t) % 16

        @pl.when(t == 0)
        def _():
            ref = landed1.at[grp, pl.ds(0, 7)]
            pltpu.make_async_copy(ref, ref, rsem1.at[t]).wait()

        @pl.when(t != 0)
        def _():
            ref = landed1.at[grp]
            pltpu.make_async_copy(ref, ref, rsem1.at[t]).wait()

        for i in range(4):
            v0 = landed1[grp, i].reshape(hk, width).astype(F32)
            v1 = landed1[grp, 4 + i].reshape(hk, width).astype(F32)
            xbuf[i * 2 * PAD:i * 2 * PAD + hk, :] = jnp.where(low32, v0, pltpu.roll(v1, 32, 1))
            xbuf[i * 2 * PAD + PAD:i * 2 * PAD + PAD + hk, :] = jnp.where(
                low32, pltpu.roll(v0, 96, 1), v1
            )
        value = xbuf[...]
        stacked = jnp.concatenate([value.astype(BF), times_i(value).astype(BF)], axis=0)
        ytab[pl.ds(pl.multiple_of(grp * 144, 8), 144), :] = dot(yf_ref[...], stacked)
        return carry

    lax.fori_loop(0, 16, arrive1, 0)

    swap = pltpu.make_async_remote_copy(
        src_ref=green_ref, dst_ref=partner, send_sem=psem, recv_sem=qsem,
        device_id=(ka, orbital * 2 + 1 - half), device_id_type=MESH,
    )
    swap.start()

    together = 6

    def distances(step, carry):
        near_in = []
        for u in range(0, together, 2):
            sides = []
            for v in range(2):
                ry = step * together + u + v
                value = ytab[pl.ds(ry, 48, stride=48), :]
                sides.append(
                    jnp.concatenate([value.astype(BF), times_i(value).astype(BF)], axis=0)
                )
            out = dot(xf_ref[...], jnp.concatenate(sides, axis=1)).astype(BF)
            near_in += [out[:, :128], out[:, 128:]]
        near_in = jnp.concatenate(near_in, axis=0)
        near = dot(jnp.concatenate([near_in, near_in], axis=1), tb[...])
        far_parts = []
        for u in range(together):
            ry = step * together + u
            w_re = wre_full[pl.ds(ry, 48, stride=48), :]
            w_im = wim_full[pl.ds(ry, 48, stride=48), :]
            n_re, n_im = near[u * 48:u * 48 + 48, :128], near[u * 48:u * 48 + 48, 128:]
            far_re = -(n_re * w_im + n_im * w_re)
            far_im = n_re * w_re - n_im * w_im
            far_parts.append(jnp.concatenate([far_re.astype(BF), far_im.astype(BF)], axis=1))
        far = jnp.concatenate(far_parts, axis=0)
        home = dot(far, pb[0:256, :]) + dot(far, pb[256:512, :])
        for u in range(0, together, 2):
            sides = []
            for v in range(2):
                value = home[(u + v) * 48:(u + v) * 48 + 48, :]
                sides.append(
                    jnp.concatenate([value.astype(BF), times_i(value).astype(BF)], axis=0)
                )
            out = dot(xi_ref[...], jnp.concatenate(sides, axis=1))
            for v in range(2):
                at = pl.multiple_of((step * together + u + v) * 48, 8)
                utab[pl.ds(at, 48), :] = out[:, v * 128:v * 128 + 128]
        return carry

    lax.fori_loop(0, 48 // together, distances, 0)

    def send2(t, carry):
        grp = (mine + t) % 16
        value = jnp.concatenate(
            [utab[pl.ds(grp * 3 + u, 48, stride=48), :] for u in range(3)], axis=0
        )
        stacked = jnp.concatenate([value.astype(BF), times_i(value).astype(BF)], axis=0)
        out = dot(yi_ref[...], stacked)
        for i in range(4):
            v0 = out[i * 2 * PAD:i * 2 * PAD + PAD]
            v1 = out[i * 2 * PAD + PAD:i * 2 * PAD + 2 * PAD]
            first = jnp.where(low32, v0, pltpu.roll(v1, 32, 1))
            second = jnp.where(low32, pltpu.roll(v0, 96, 1), v1)
            packed2[grp, i] = first[:hk].astype(BF).reshape(hk // 2, 2, width)
            packed2[grp, 4 + i] = second[:hk].astype(BF).reshape(hk // 2, 2, width)
        for slot in range(8):
            @pl.when((t != 0) | (slot != place))
            def _():
                pltpu.make_async_remote_copy(
                    src_ref=packed2.at[grp, slot], dst_ref=landed2.at[mine, place],
                    send_sem=ssem2, recv_sem=rsem2.at[t],
                    device_id=device_of(grp, slot), device_id_type=MESH,
                ).start()
        return carry

    lax.fori_loop(0, 16, send2, 0)
    own2 = pltpu.make_async_copy(packed2.at[mine, place], landed2.at[mine, place], lsem)
    own2.start()

    swap.wait()
    mine_at = pl.multiple_of(half * rows_m, 32)
    other_at = pl.multiple_of((1 - half) * rows_m, 32)

    def build(k, carry):
        for ref, at in ((green_ref, mine_at), (partner, other_at)):
            value = ref[k]
            turned = (pltpu.roll(value.astype(F32), 64, 1) * -minus_low).astype(BF)
            gmat[k, pl.ds(at, rows_m), :] = turned
            gmat[k, pl.ds(64 + at, rows_m), :] = value
        return carry

    lax.fori_loop(0, count_k, build, 0)
    own2.wait()

    def arrive2(t, carry):
        grp = (mine + 16 - t) % 16

        @pl.when(t == 0)
        def _():
            ref = landed2.at[grp, pl.ds(0, 7)]
            pltpu.make_async_copy(ref, ref, rsem2.at[t]).wait()

        @pl.when(t != 0)
        def _():
            ref = landed2.at[grp]
            pltpu.make_async_copy(ref, ref, rsem2.at[t]).wait()

        for slot in range(8):
            value = landed2[grp, slot].reshape(hk, width).astype(F32)
            start = pl.multiple_of((grp * 8 + slot) * PAD, 8)
            pages[pl.ds(start, hk), :] = value
        return carry

    lax.fori_loop(0, 16, arrive2, 0)

    for r in range(hk):
        value = pages[pl.ds(r, 128, stride=PAD), :].T.astype(BF)
        for k2 in range(2):
            amat[(k2 * hk + r) * rows_m:(k2 * hk + r + 1) * rows_m, 0:128] = value[
                k2 * 32:k2 * 32 + 32
            ]
            amat[(k2 * hk + r) * rows_m:(k2 * hk + r + 1) * rows_m, 128:256] = value[
                64 + k2 * 32:64 + k2 * 32 + 32
            ]

    def coeffs(i, carry):
        at = pl.multiple_of(i * 192, 32)
        value = amat[pl.ds(at, 192), :]
        sigma = (dot(value, pq[0:256, :]) + dot(value, pq[256:512, :])).astype(BF)
        sigma_ref[pl.ds(i * 6, 6)] = sigma.reshape(6, rows_m, width)
        skm[pl.ds(at, 192), :] = dot(jnp.concatenate([sigma, sigma], axis=1), kb[...]).astype(BF)
        for u in range(6):
            k = i * 6 + u
            row = pl.multiple_of(i * 192 + u * 32, 32)
            memory = dot(skm[pl.ds(row, rows_m), :], gmat[k])
            turned = gmat[k, pl.ds(mine_at, rows_m), :].astype(F32)
            own = green_ref[k].astype(F32)
            energy = energy_ref[orbital, k]
            next_ref[k] = (own + STEP_SIZE * (energy * turned + memory)).astype(BF)
        return carry

    lax.fori_loop(0, count_k // 6, coeffs, 0)

    ref = landed1.at[pl.ds(0, 15)]
    pltpu.make_async_copy(ref, ref, ssem1).wait()
    ref = landed1.at[0, pl.ds(0, 7)]
    pltpu.make_async_copy(ref, ref, ssem1).wait()
    ref = landed2.at[pl.ds(0, 15)]
    pltpu.make_async_copy(ref, ref, ssem2).wait()
    ref = landed2.at[0, pl.ds(0, 7)]
    pltpu.make_async_copy(ref, ref, ssem2).wait()


def on_device(green_coeff, screened, band_energy, time_basis, projector, memory_kernel):
    total_k = screened.shape[0]
    tables = [jnp.asarray(t, BF) for t in phase_tables(48, green_coeff.shape[0], 4)]
    vmem = pl.BlockSpec(memory_space=pltpu.VMEM)
    dma = pltpu.SemaphoreType.DMA
    message = (16, 8, 9, 2, 128)
    out = jax.ShapeDtypeStruct(green_coeff.shape, BF)
    return pl.pallas_call(
        kernel,
        out_shape=(out, out),
        in_specs=[
            vmem,
            pl.BlockSpec(memory_space=pl.ANY),
            pl.BlockSpec(memory_space=pltpu.SMEM),
            vmem, vmem, vmem, vmem, vmem, vmem, vmem,
        ],
        out_specs=(vmem, vmem),
        scratch_shapes=[
            pltpu.VMEM((total_k, 256), BF),
            pltpu.VMEM((total_k, 128), F32),
            pltpu.VMEM((total_k, 128), F32),
            pltpu.VMEM((128 * PAD, 128), F32),
            pltpu.VMEM(message, BF),
            pltpu.VMEM(message, BF),
            pltpu.VMEM(message, BF),
            pltpu.VMEM(message, BF),
            pltpu.VMEM((total_k, 128), F32),
            pltpu.VMEM((total_k, 128), F32),
            pltpu.VMEM((8 * PAD, 128), F32),
            pltpu.VMEM((256, 256), BF),
            pltpu.VMEM((512, 128), BF),
            pltpu.VMEM((512, 128), BF),
            pltpu.VMEM((256, 128), BF),
            pltpu.VMEM((256, 128), F32),
            pltpu.VMEM(green_coeff.shape, BF),
            pltpu.VMEM((36, 128, 128), BF),
            pltpu.VMEM((1152, 256), BF),
            pltpu.VMEM((1152, 128), BF),
            dma, dma, dma, dma((16,)), dma, dma((16,)), dma, dma,
        ],
        compiler_params=pltpu.CompilerParams(
            collective_id=0, has_side_effects=True, vmem_limit_bytes=48 * 2**20
        ),
    )(
        green_coeff,
        screened.reshape(total_k, 256),
        band_energy.T,
        time_basis,
        projector.T,
        memory_kernel,
        *tables,
    )


def solution(mesh):
    return jax.shard_map(
        on_device,
        mesh=mesh,
        in_specs=(P("ka", "ot", None), P(None, ("ot", "ka"), None), P("ka", None), P(), P(), P()),
        out_specs=(P("ka", "ot", None), P("ka", "ot", None)),
        check_vma=False,
    )
```

profile of v0, /device:TPU:1, one launch (start us, length us, event | category | flops | bytes accessed | tf_op | source)
XLA Modules:
  0.0 71.3 jit_solution(7986454010214830224)
XLA Ops:
  0.6 0.0 copy-start
  0.6 1.3 %copy-done = bf16[2304,1,256]{2,0,1:T(8,128)(2,1)S(1)} copy-done((bf16[2304,1,256]{2,0,1:T(8,128)(2,1)S(1)}, bf16[2304,1,256]{2,0,1:T(8,128)(2,1)}, u32[]{:S(2)}) %copy-start) | copy-done | bytes 1179672
  1.9 0.0 copy-start.1
  1.9 1.0 %copy-done.1 = bf16[36,32,128]{2,1,0:T(8,128)(2,1)S(1)} copy-done((bf16[36,32,128]{2,1,0:T(8,128)(2,1)S(1)}, bf16[36,32,128]{2,1,0:T(8,128)(2,1)}, u32[]{:S(2)}) %copy-start.1) | copy-done | bytes 294936
  2.9 0.0 copy-start.2
  2.9 0.9 %copy-done.2 = bf16[192,288]{1,0:T(8,128)(2,1)S(1)} copy-done((bf16[192,288]{1,0:T(8,128)(2,1)S(1)}, bf16[192,288]{1,0:T(8,128)(2,1)}, u32[]{:S(2)}) %copy-start.2) | copy-done | bytes 110616
  3.8 0.0 copy-start.3
  3.8 0.9 %copy-done.3 = bf16[144,384]{1,0:T(8,128)(2,1)S(1)} copy-done((bf16[144,384]{1,0:T(8,128)(2,1)S(1)}, bf16[144,384]{1,0:T(8,128)(2,1)}, u32[]{:S(2)}) %copy-start.3) | copy-done | bytes 110616
  4.7 0.0 copy-start.4
  4.7 0.8 %copy-done.4 = f32[64,128]{1,0:T(8,128)S(1)} copy-done((f32[64,128]{1,0:T(8,128)S(1)}, f32[64,128]{1,0:T(8,128)}, u32[]{:S(2)}) %copy-start.4) | copy-done | bytes 32792
  5.4 0.0 copy-start.5
  5.4 0.8 %copy-done.5 = f32[128,64]{0,1:T(8,128)S(1)} copy-done((f32[128,64]{0,1:T(8,128)S(1)}, f32[128,64]{0,1:T(8,128)}, u32[]{:S(2)}) %copy-start.5) | copy-done | bytes 32792
  6.2 0.0 copy-start.6
  6.2 0.8 %copy-done.6 = f32[64,64]{1,0:T(8,128)S(1)} copy-done((f32[64,64]{1,0:T(8,128)S(1)}, f32[64,64]{1,0:T(8,128)}, u32[]{:S(2)}) %copy-start.6) | copy-done | bytes 16408
  6.9 0.0 copy-start.7
  7.0 0.7 copy-done.7
  7.7 0.0 copy-start.8
  7.7 0.7 copy-done.8
  8.4 0.0 copy-start.9
  8.4 0.7 copy-done.9
  9.0 60.9 %shard_map.113 = (bf16[36,32,128]{2,1,0:T(8,128)(2,1)S(1)}, bf16[36,32,128]{2,1,0:T(8,128)(2,1)S(1)}) custom-call(bf16[36,32,128]{2,1,0:T(8,128)(2,1)S(1)} %copy-done.1, bf16[2304,256]{1,0:T(8,128)(2,1)S(1)} %bitcast.3, f32[2,36]{1,0:T(2,128)S(1)} %bitcast.5, f32[64,128]{1,0:T(8,128)S(1)} %copy-done.4, f32[64,128]{1,0:T(8,128)S(1)} %bitcast.4, ...), custom_call_target="tpu_custom_call" | custom-call | tf_op jit(solution)/shard_map/pallas_call | solution.py:365
  69.9 0.7 %copy.14 = bf16[36,32,128]{2,1,0:T(8,128)(2,1)} copy(bf16[36,32,128]{2,1,0:T(8,128)(2,1)S(1)} %get-tuple-element.4) | data formatting | bytes 589824
  70.6 0.7 copy.15
Async XLA Ops:
  0.6 1.3 %copy-start = (bf16[2304,1,256]{2,0,1:T(8,128)(2,1)S(1)}, bf16[2304,1,256]{2,0,1:T(8,128)(2,1)}, u32[]{:S(2)}) copy-start(bf16[2304,1,256]{2,0,1:T(8,128)(2,1)} %param.11) | copy-start | bytes 3538948
  1.9 1.0 %copy-start.1 = (bf16[36,32,128]{2,1,0:T(8,128)(2,1)S(1)}, bf16[36,32,128]{2,1,0:T(8,128)(2,1)}, u32[]{:S(2)}) copy-start(bf16[36,32,128]{2,1,0:T(8,128)(2,1)} %green_ref.1) | copy-start | bytes 884740
  2.9 0.9 %copy-start.2 = (bf16[192,288]{1,0:T(8,128)(2,1)S(1)}, bf16[192,288]{1,0:T(8,128)(2,1)}, u32[]{:S(2)}) copy-start(bf16[192,288]{1,0:T(8,128)(2,1)} %constant.11.clone.yi_ref) | copy-start | bytes 331780
  3.8 0.9 %copy-start.3 = (bf16[144,384]{1,0:T(8,128)(2,1)S(1)}, bf16[144,384]{1,0:T(8,128)(2,1)}, u32[]{:S(2)}) copy-start(bf16[144,384]{1,0:T(8,128)(2,1)} %constant.10.clone.yf_ref) | copy-start | bytes 331780
  4.7 0.8 %copy-start.4 = (f32[64,128]{1,0:T(8,128)S(1)}, f32[64,128]{1,0:T(8,128)}, u32[]{:S(2)}) copy-start(f32[64,128]{1,0:T(8,128)} %basis_ref.1) | copy-start | bytes 98308
  5.4 0.8 %copy-start.5 = (f32[128,64]{0,1:T(8,128)S(1)}, f32[128,64]{0,1:T(8,128)}, u32[]{:S(2)}) copy-start(f32[128,64]{0,1:T(8,128)} %param.14) | copy-start | bytes 98308
  6.2 0.8 %copy-start.6 = (f32[64,64]{1,0:T(8,128)S(1)}, f32[64,64]{1,0:T(8,128)}, u32[]{:S(2)}) copy-start(f32[64,64]{1,0:T(8,128)} %memk_ref.1) | copy-start | bytes 49156
  6.9 0.7 copy-start.7
  7.7 0.7 copy-start.8
  8.4 0.7 copy-start.9
where the time goes:
time: 72.3 us; the launch traced here: 71.3 us
  Pallas kernels  60.9 us (84%)
  local copies, waits for them, and re-layouts  9.82 us (14%)
    pallas_call x1, Pallas kernels, on_device(): pl.pallas_call(kernel, out_shape=(out, out), in_specs=[vmem, pl.BlockSpec...  60.9 us
    unnamed x22, local copies, waits for them, and re-layouts  9.82 us

commit v1 on v0

--- a/solution.py
+++ b/solution.py
@@ -50,12 +50,12 @@
 
 
 def kernel(
-    green_ref, screen_ref, energy_ref, basis_ref, proj_ref, memk_ref,
-    xf_ref, xi_ref, yf_ref, yi_ref,
+    green_in, screen_in, energy_in, basis_in, proj_in, memk_in, xf_in, xi_in, yf_in, yi_in,
     sigma_ref, next_ref,
-    w_raw, wre_full, wim_full, pages, packed1, landed1, packed2, landed2, ytab, utab, xbuf,
+    green_ref, w_raw, energy_ref, basis_ref, proj_ref, memk_ref, xf_ref, xi_ref, yf_ref, yi_ref,
+    fsem, wre_full, wim_full, pages, packed1, landed1, packed2, landed2, ytab, utab, xbuf,
     tb, pb, pq, kb, pt, partner, gmat, amat, skm,
-    wsem, lsem, ssem1, rsem1, ssem2, rsem2, psem, qsem,
+    lsem, ssem1, rsem1, ssem2, rsem2, psem, qsem,
 ):
     ka, ot = lax.axis_index("ka"), lax.axis_index("ot")
     half, orbital = ot % 2, ot // 2
@@ -74,9 +74,19 @@
         pl.semaphore_signal(barrier, inc=1, device_id=device_of(grp, slot), device_id_type=MESH)
         return carry
 
+    fetches = [
+        pltpu.make_async_copy(source, target, fsem.at[i])
+        for i, (source, target) in enumerate([
+            (green_in, green_ref), (basis_in, basis_ref), (screen_in, w_raw),
+            (energy_in, energy_ref), (proj_in, proj_ref), (memk_in, memk_ref),
+            (xf_in, xf_ref), (xi_in, xi_ref), (yf_in, yf_ref), (yi_in, yi_ref),
+        ])
+    ]
+    for fetch in fetches:
+        fetch.start()
     lax.fori_loop(1, 128, greet, 0)
-    w_copy = pltpu.make_async_copy(screen_ref, w_raw, wsem)
-    w_copy.start()
+    for fetch in fetches[:2]:
+        fetch.wait()
 
     lane64 = lax.broadcasted_iota(jnp.int32, (1, width), 1)
     low64 = lane64 < 64
@@ -131,6 +141,8 @@
     own1 = pltpu.make_async_copy(packed1.at[mine, place], landed1.at[mine, place], lsem)
     own1.start()
 
+    for fetch in fetches[2:]:
+        fetch.wait()
     zeros = jnp.zeros((64, 128), F32)
     basis = basis_ref[...]
     wide = jnp.concatenate(
@@ -164,7 +176,6 @@
     high, low = split(wide)
     kb[0:128, :] = high
     kb[128:256, :] = low
-    w_copy.wait()
     scale = 1.0 / w_raw.shape[0]
 
     def widen(i, carry):
@@ -361,19 +372,21 @@
     vmem = pl.BlockSpec(memory_space=pltpu.VMEM)
     dma = pltpu.SemaphoreType.DMA
     message = (16, 8, 9, 2, 128)
-    out = jax.ShapeDtypeStruct(green_coeff.shape, BF)
+    out = pltpu.VMEM(green_coeff.shape, BF)
     return pl.pallas_call(
         kernel,
         out_shape=(out, out),
-        in_specs=[
-            vmem,
-            pl.BlockSpec(memory_space=pl.ANY),
-            pl.BlockSpec(memory_space=pltpu.SMEM),
-            vmem, vmem, vmem, vmem, vmem, vmem, vmem,
-        ],
+        in_specs=[pl.BlockSpec(memory_space=pl.ANY)] * 10,
         out_specs=(vmem, vmem),
         scratch_shapes=[
+            pltpu.VMEM(green_coeff.shape, BF),
             pltpu.VMEM((total_k, 256), BF),
+            pltpu.SMEM((2, green_coeff.shape[0]), F32),
+            pltpu.VMEM(time_basis.shape, F32),
+            pltpu.VMEM(time_basis.shape, F32),
+            pltpu.VMEM(memory_kernel.shape, F32),
+            *[pltpu.VMEM(t.shape, BF) for t in tables],
+            dma((10,)),
             pltpu.VMEM((total_k, 128), F32),
             pltpu.VMEM((total_k, 128), F32),
             pltpu.VMEM((128 * PAD, 128), F32),
@@ -393,10 +406,10 @@
             pltpu.VMEM((36, 128, 128), BF),
             pltpu.VMEM((1152, 256), BF),
             pltpu.VMEM((1152, 128), BF),
-            dma, dma, dma, dma((16,)), dma, dma((16,)), dma, dma,
+            dma, dma, dma((16,)), dma, dma((16,)), dma, dma,
         ],
         compiler_params=pltpu.CompilerParams(
-            collective_id=0, has_side_effects=True, vmem_limit_bytes=48 * 2**20
+            collective_id=0, has_side_effects=True, vmem_limit_bytes=60 * 2**20
         ),
     )(
         green_coeff,

time: 72.3 us -> 63.1 us (0.87)
  local copies, waits for them, and re-layouts: 9.82 us -> 1.43 us
    unnamed x22 -> x2, local copies, waits for them, and re-layouts: 9.82 us -> 1.43 us
where the time goes in v1:
time: 63.1 us; the launch traced here: 62.5 us
  Pallas kernels  60.4 us (96%)
  local copies, waits for them, and re-layouts  1.43 us (2%)
  between operations  0.64 us (1%)
    pallas_call x1, Pallas kernels, on_device(): pl.pallas_call(kernel, out_shape=(out, out), in_specs=[pl.BlockSpec(memor...  60.4 us
    unnamed x2, local copies, waits for them, and re-layouts  1.43 us

profile of v1, /device:TPU:1, one launch (start us, length us, event | category | flops | bytes accessed | tf_op | source)
XLA Modules:
  0.0 62.5 jit_solution(9765263622899599854)
XLA Ops:
  0.6 60.4 %shard_map.113 = (bf16[36,32,128]{2,1,0:T(8,128)(2,1)S(1)}, bf16[36,32,128]{2,1,0:T(8,128)(2,1)S(1)}) custom-call(bf16[36,32,128]{2,1,0:T(8,128)(2,1)} %green_in.1, bf16[2304,256]{1,0:T(8,128)(2,1)} %bitcast.3, f32[2,36]{1,0:T(2,128)} %bitcast.5, f32[64,128]{1,0:T(8,128)} %basis_in.1, f32[64,128]{1,0:T(8,128)} %bitcast.4, f32[64,64]{1,0:T(8,128)} %memk_in.1, ...), custom_call_target="tpu_custom_call" | custom-call | tf_op jit(solution)/shard_map/pallas_call | solution.py:376
  61.1 0.7 %copy.14 = bf16[36,32,128]{2,1,0:T(8,128)(2,1)} copy(bf16[36,32,128]{2,1,0:T(8,128)(2,1)S(1)} %get-tuple-element.2) | data formatting | bytes 589824
  61.8 0.7 %copy.15 = bf16[36,32,128]{2,1,0:T(8,128)(2,1)} copy(bf16[36,32,128]{2,1,0:T(8,128)(2,1)S(1)} %get-tuple-element.3) | data formatting | bytes 589824

commit v2 on v1

--- a/solution.py
+++ b/solution.py
@@ -53,7 +53,7 @@
     green_in, screen_in, energy_in, basis_in, proj_in, memk_in, xf_in, xi_in, yf_in, yi_in,
     sigma_ref, next_ref,
     green_ref, w_raw, energy_ref, basis_ref, proj_ref, memk_ref, xf_ref, xi_ref, yf_ref, yi_ref,
-    fsem, wre_full, wim_full, pages, packed1, landed1, packed2, landed2, ytab, utab, xbuf,
+    fsem, plane_in, wre_full, wim_full, pages, packed1, landed1, packed2, landed2, ytab, utab, xbuf,
     tb, pb, pq, kb, pt, partner, gmat, amat, skm,
     lsem, ssem1, rsem1, ssem2, rsem2, psem, qsem,
 ):
@@ -68,11 +68,8 @@
 
     barrier = pltpu.get_barrier_semaphore()
 
-    def greet(step, carry):
-        slot = (place + step) % 8
-        grp = (mine + step // 8) % 16
-        pl.semaphore_signal(barrier, inc=1, device_id=device_of(grp, slot), device_id_type=MESH)
-        return carry
+    def tell(semaphore, grp, slot):
+        pl.semaphore_signal(semaphore, inc=1, device_id=device_of(grp, slot), device_id_type=MESH)
 
     fetches = [
         pltpu.make_async_copy(source, target, fsem.at[i])
@@ -84,9 +81,26 @@
     ]
     for fetch in fetches:
         fetch.start()
-    lax.fori_loop(1, 128, greet, 0)
+    for s in range(1, 16):
+        tell(barrier, mine ^ s, place)
+    for s in range(1, 8):
+        tell(barrier, mine, place ^ s)
+    pl.semaphore_wait(barrier, 22)
+    for s in range(1, 8):
+        tell(plane_in, mine, place ^ s)
     for fetch in fetches[:2]:
         fetch.wait()
+
+
+    def swap(part):
+        lo, hi = ((0, 18), (18, count_k))[part]
+        return pltpu.make_async_remote_copy(
+            src_ref=green_ref.at[pl.ds(lo, hi - lo)], dst_ref=partner.at[pl.ds(lo, hi - lo)],
+            send_sem=psem.at[part], recv_sem=qsem.at[part],
+            device_id=(ka, orbital * 2 + 1 - half), device_id_type=MESH,
+        )
+
+    swap(0).start()
 
     lane64 = lax.broadcasted_iota(jnp.int32, (1, width), 1)
     low64 = lane64 < 64
@@ -118,7 +132,7 @@
     for r in range(hk):
         rows_step(r, 0)
 
-    pl.semaphore_wait(barrier, 127)
+    pl.semaphore_wait(plane_in, 7)
 
     def send1(t, carry):
         grp = (mine + t) % 16
@@ -179,13 +193,12 @@
     scale = 1.0 / w_raw.shape[0]
 
     def widen(i, carry):
-        at = pl.ds(pl.multiple_of(i * 96, 32), 96)
-        value = w_raw[at, :].astype(F32) * scale
-        wre_full[at, :] = value[:, :128]
-        wim_full[at, :] = value[:, 128:]
-        return carry
-
-    lax.fori_loop(0, 24, widen, 0)
+        value = w_raw[pl.ds(pl.multiple_of(i * 48, 16), 48), :].astype(F32) * scale
+        wre_full[pl.ds(i, 48, stride=48), :] = value[:, :128]
+        wim_full[pl.ds(i, 48, stride=48), :] = value[:, 128:]
+        return carry
+
+    lax.fori_loop(0, 48, widen, 0)
     xbuf[...] = jnp.zeros_like(xbuf)
     own1.wait()
 
@@ -211,18 +224,16 @@
             )
         value = xbuf[...]
         stacked = jnp.concatenate([value.astype(BF), times_i(value).astype(BF)], axis=0)
-        ytab[pl.ds(pl.multiple_of(grp * 144, 8), 144), :] = dot(yf_ref[...], stacked)
+        out = dot(yf_ref[...], stacked)
+        for u in range(3):
+            ytab[pl.ds(grp * 3 + u, 48, stride=48), :] = out[u * 48:u * 48 + 48]
         return carry
 
     lax.fori_loop(0, 16, arrive1, 0)
 
-    swap = pltpu.make_async_remote_copy(
-        src_ref=green_ref, dst_ref=partner, send_sem=psem, recv_sem=qsem,
-        device_id=(ka, orbital * 2 + 1 - half), device_id_type=MESH,
-    )
-    swap.start()
-
-    together = 6
+    swap(1).start()
+
+    together = 12
 
     def distances(step, carry):
         near_in = []
@@ -230,7 +241,7 @@
             sides = []
             for v in range(2):
                 ry = step * together + u + v
-                value = ytab[pl.ds(ry, 48, stride=48), :]
+                value = ytab[pl.ds(pl.multiple_of(ry * 48, 8), 48), :]
                 sides.append(
                     jnp.concatenate([value.astype(BF), times_i(value).astype(BF)], axis=0)
                 )
@@ -241,8 +252,8 @@
         far_parts = []
         for u in range(together):
             ry = step * together + u
-            w_re = wre_full[pl.ds(ry, 48, stride=48), :]
-            w_im = wim_full[pl.ds(ry, 48, stride=48), :]
+            w_re = wre_full[pl.ds(pl.multiple_of(ry * 48, 8), 48), :]
+            w_im = wim_full[pl.ds(pl.multiple_of(ry * 48, 8), 48), :]
             n_re, n_im = near[u * 48:u * 48 + 48, :128], near[u * 48:u * 48 + 48, 128:]
             far_re = -(n_re * w_im + n_im * w_re)
             far_im = n_re * w_re - n_im * w_im
@@ -292,7 +303,8 @@
     own2 = pltpu.make_async_copy(packed2.at[mine, place], landed2.at[mine, place], lsem)
     own2.start()
 
-    swap.wait()
+    swap(0).wait()
+    swap(1).wait()
     mine_at = pl.multiple_of(half * rows_m, 32)
     other_at = pl.multiple_of((1 - half) * rows_m, 32)
 
@@ -339,14 +351,14 @@
             ]
 
     def coeffs(i, carry):
-        at = pl.multiple_of(i * 192, 32)
-        value = amat[pl.ds(at, 192), :]
+        at = pl.multiple_of(i * 384, 32)
+        value = amat[pl.ds(at, 384), :]
         sigma = (dot(value, pq[0:256, :]) + dot(value, pq[256:512, :])).astype(BF)
-        sigma_ref[pl.ds(i * 6, 6)] = sigma.reshape(6, rows_m, width)
-        skm[pl.ds(at, 192), :] = dot(jnp.concatenate([sigma, sigma], axis=1), kb[...]).astype(BF)
-        for u in range(6):
-            k = i * 6 + u
-            row = pl.multiple_of(i * 192 + u * 32, 32)
+        sigma_ref[pl.ds(i * 12, 12)] = sigma.reshape(12, rows_m, width)
+        skm[pl.ds(at, 384), :] = dot(jnp.concatenate([sigma, sigma], axis=1), kb[...]).astype(BF)
+        for u in range(12):
+            k = i * 12 + u
+            row = pl.multiple_of(i * 384 + u * 32, 32)
             memory = dot(skm[pl.ds(row, rows_m), :], gmat[k])
             turned = gmat[k, pl.ds(mine_at, rows_m), :].astype(F32)
             own = green_ref[k].astype(F32)
@@ -354,7 +366,7 @@
             next_ref[k] = (own + STEP_SIZE * (energy * turned + memory)).astype(BF)
         return carry
 
-    lax.fori_loop(0, count_k // 6, coeffs, 0)
+    lax.fori_loop(0, count_k // 12, coeffs, 0)
 
     ref = landed1.at[pl.ds(0, 15)]
     pltpu.make_async_copy(ref, ref, ssem1).wait()
@@ -387,6 +399,7 @@
             pltpu.VMEM(memory_kernel.shape, F32),
             *[pltpu.VMEM(t.shape, BF) for t in tables],
             dma((10,)),
+            pltpu.SemaphoreType.REGULAR,
             pltpu.VMEM((total_k, 128), F32),
             pltpu.VMEM((total_k, 128), F32),
             pltpu.VMEM((128 * PAD, 128), F32),
@@ -406,7 +419,7 @@
             pltpu.VMEM((36, 128, 128), BF),
             pltpu.VMEM((1152, 256), BF),
             pltpu.VMEM((1152, 128), BF),
-            dma, dma, dma((16,)), dma, dma((16,)), dma, dma,
+            dma, dma, dma((16,)), dma, dma((16,)), dma((2,)), dma((2,)),
         ],
         compiler_params=pltpu.CompilerParams(
             collective_id=0, has_side_effects=True, vmem_limit_bytes=60 * 2**20

time: 63.1 us -> 57.4 us (0.910)
  Pallas kernels: 60.4 us -> 55.3 us
    pallas_call x1, Pallas kernels: 60.4 us -> 55.3 us  [on_device(): pl.pallas_call(kernel, out_shape=(out, out), in_specs=[pl.BlockSpec(memor...]
where the time goes in v2:
time: 57.4 us
  Pallas kernels  55.3 us (96%)
  local copies, waits for them, and re-layouts  1.43 us (2%)
  between operations  0.64 us (1%)
    pallas_call x1, Pallas kernels, on_device(): pl.pallas_call(kernel, out_shape=(out, out), in_specs=[pl.BlockSpec(memor...  55.3 us
    unnamed x2, local copies, waits for them, and re-layouts  1.43 us

profile of v2, /device:TPU:1, one launch (start us, length us, event | category | flops | bytes accessed | tf_op | source)
XLA Modules:
  0.0 57.4 jit_solution(3465407109841888307)
XLA Ops:
  0.6 55.3 %shard_map.113 = (bf16[36,32,128]{2,1,0:T(8,128)(2,1)S(1)}, bf16[36,32,128]{2,1,0:T(8,128)(2,1)S(1)}) custom-call(bf16[36,32,128]{2,1,0:T(8,128)(2,1)} %green_in.1, bf16[2304,256]{1,0:T(8,128)(2,1)} %bitcast.3, f32[2,36]{1,0:T(2,128)} %bitcast.5, f32[64,128]{1,0:T(8,128)} %basis_in.1, f32[64,128]{1,0:T(8,128)} %bitcast.4, f32[64,64]{1,0:T(8,128)} %memk_in.1, ...), custom_call_target="tpu_custom_call" | custom-call | tf_op jit(solution)/shard_map/pallas_call | solution.py:388
  55.9 0.7 %copy.14 = bf16[36,32,128]{2,1,0:T(8,128)(2,1)} copy(bf16[36,32,128]{2,1,0:T(8,128)(2,1)S(1)} %get-tuple-element.2) | data formatting | bytes 589824
  56.6 0.7 %copy.15 = bf16[36,32,128]{2,1,0:T(8,128)(2,1)} copy(bf16[36,32,128]{2,1,0:T(8,128)(2,1)S(1)} %get-tuple-element.3) | data formatting | bytes 589824

commit v3 on v2

--- a/solution.py
+++ b/solution.py
@@ -23,7 +23,7 @@
     sine = lambda a, b: np.sin(2.0 * math.pi * (a * b % lattice) / lattice)
     idx = np.arange(lattice)
     cx, sx = cosine(idx[:, None], idx[None, :]), sine(idx[:, None], idx[None, :])
-    x_fwd = np.concatenate([cx, sx], axis=1)
+    x_fwd = np.kron(np.eye(3), np.concatenate([cx, sx], axis=0))
     x_inv = np.concatenate([cx, -sx], axis=1)
     row = np.arange(group * 2 * PAD)
     place, inner = row // PAD, row % PAD
@@ -233,20 +233,30 @@
 
     swap(1).start()
 
-    together = 12
+    together = 24
+
+    def along_x(values, sign):
+        done = []
+        for u in range(0, len(values), 2 * 3):
+            sides = [
+                jnp.concatenate([v.astype(BF) for v in values[at:at + 3]], axis=0)
+                for at in (u, u + 3)
+            ]
+            out = dot(xf_ref[...], jnp.concatenate(sides, axis=1))
+            for v in range(2):
+                for at in range(0, 96 * 3, 96):
+                    even = out[at:at + 48, v * 128:v * 128 + 128]
+                    odd = out[at + 48:at + 96, v * 128:v * 128 + 128]
+                    done.append(even + pltpu.roll(odd, 64, 1) * (minus_low * sign))
+        return done
+
 
     def distances(step, carry):
-        near_in = []
-        for u in range(0, together, 2):
-            sides = []
-            for v in range(2):
-                ry = step * together + u + v
-                value = ytab[pl.ds(pl.multiple_of(ry * 48, 8), 48), :]
-                sides.append(
-                    jnp.concatenate([value.astype(BF), times_i(value).astype(BF)], axis=0)
-                )
-            out = dot(xf_ref[...], jnp.concatenate(sides, axis=1)).astype(BF)
-            near_in += [out[:, :128], out[:, 128:]]
+        near_in = along_x(
+            [ytab[pl.ds(pl.multiple_of((step * together + u) * 48, 8), 48), :] for u in range(together)],
+            1.0,
+        )
+        near_in = [v.astype(BF) for v in near_in]
         near_in = jnp.concatenate(near_in, axis=0)
         near = dot(jnp.concatenate([near_in, near_in], axis=1), tb[...])
         far_parts = []
@@ -260,17 +270,9 @@
             far_parts.append(jnp.concatenate([far_re.astype(BF), far_im.astype(BF)], axis=1))
         far = jnp.concatenate(far_parts, axis=0)
         home = dot(far, pb[0:256, :]) + dot(far, pb[256:512, :])
-        for u in range(0, together, 2):
-            sides = []
-            for v in range(2):
-                value = home[(u + v) * 48:(u + v) * 48 + 48, :]
-                sides.append(
-                    jnp.concatenate([value.astype(BF), times_i(value).astype(BF)], axis=0)
-                )
-            out = dot(xi_ref[...], jnp.concatenate(sides, axis=1))
-            for v in range(2):
-                at = pl.multiple_of((step * together + u + v) * 48, 8)
-                utab[pl.ds(at, 48), :] = out[:, v * 128:v * 128 + 128]
+        back = along_x([home[u * 48:u * 48 + 48, :] for u in range(together)], -1.0)
+        for u in range(together):
+            utab[pl.ds(pl.multiple_of((step * together + u) * 48, 8), 48), :] = back[u]
         return carry
 
     lax.fori_loop(0, 48 // together, distances, 0)
@@ -351,14 +353,14 @@
             ]
 
     def coeffs(i, carry):
-        at = pl.multiple_of(i * 384, 32)
-        value = amat[pl.ds(at, 384), :]
+        at = pl.multiple_of(i * 1152, 32)
+        value = amat[pl.ds(at, 1152), :]
         sigma = (dot(value, pq[0:256, :]) + dot(value, pq[256:512, :])).astype(BF)
-        sigma_ref[pl.ds(i * 12, 12)] = sigma.reshape(12, rows_m, width)
-        skm[pl.ds(at, 384), :] = dot(jnp.concatenate([sigma, sigma], axis=1), kb[...]).astype(BF)
-        for u in range(12):
-            k = i * 12 + u
-            row = pl.multiple_of(i * 384 + u * 32, 32)
+        sigma_ref[pl.ds(i * 36, 36)] = sigma.reshape(36, rows_m, width)
+        skm[pl.ds(at, 1152), :] = dot(jnp.concatenate([sigma, sigma], axis=1), kb[...]).astype(BF)
+        for u in range(36):
+            k = i * 36 + u
+            row = pl.multiple_of(i * 1152 + u * 32, 32)
             memory = dot(skm[pl.ds(row, rows_m), :], gmat[k])
             turned = gmat[k, pl.ds(mine_at, rows_m), :].astype(F32)
             own = green_ref[k].astype(F32)
@@ -366,7 +368,7 @@
             next_ref[k] = (own + STEP_SIZE * (energy * turned + memory)).astype(BF)
         return carry
 
-    lax.fori_loop(0, count_k // 12, coeffs, 0)
+    lax.fori_loop(0, count_k // 36, coeffs, 0)
 
     ref = landed1.at[pl.ds(0, 15)]
     pltpu.make_async_copy(ref, ref, ssem1).wait()

time: 57.4 us -> 55.9 us (0.974)
  Pallas kernels: 55.3 us -> 53.4 us
    pallas_call x1, Pallas kernels: 55.3 us -> 53.4 us  [on_device(): pl.pallas_call(kernel, out_shape=(out, out), in_specs=[pl.BlockSpec(memor...]
where the time goes in v3:
time: 55.9 us; the launch traced here: 55.5 us
  Pallas kernels  53.4 us (96%)
  local copies, waits for them, and re-layouts  1.43 us (3%)
  between operations  0.64 us (1%)
    pallas_call x1, Pallas kernels, on_device(): pl.pallas_call(kernel, out_shape=(out, out), in_specs=[pl.BlockSpec(memor...  53.4 us
    unnamed x2, local copies, waits for them, and re-layouts  1.43 us

profile of v3, /device:TPU:1, one launch (start us, length us, event | category | flops | bytes accessed | tf_op | source)
XLA Modules:
  0.0 55.5 jit_solution(14079779456911900386)
XLA Ops:
  0.6 53.4 %shard_map.113 = (bf16[36,32,128]{2,1,0:T(8,128)(2,1)S(1)}, bf16[36,32,128]{2,1,0:T(8,128)(2,1)S(1)}) custom-call(bf16[36,32,128]{2,1,0:T(8,128)(2,1)} %green_in.1, bf16[2304,256]{1,0:T(8,128)(2,1)} %bitcast.3, f32[2,36]{1,0:T(2,128)} %bitcast.5, f32[64,128]{1,0:T(8,128)} %basis_in.1, f32[64,128]{1,0:T(8,128)} %bitcast.4, f32[64,64]{1,0:T(8,128)} %memk_in.1, ...), custom_call_target="tpu_custom_call" | custom-call | tf_op jit(solution)/shard_map/pallas_call | solution.py:390
  54.0 0.7 %copy.14 = bf16[36,32,128]{2,1,0:T(8,128)(2,1)} copy(bf16[36,32,128]{2,1,0:T(8,128)(2,1)S(1)} %get-tuple-element.2) | data formatting | bytes 589824
  54.7 0.7 %copy.15 = bf16[36,32,128]{2,1,0:T(8,128)(2,1)} copy(bf16[36,32,128]{2,1,0:T(8,128)(2,1)S(1)} %get-tuple-element.3) | data formatting | bytes 589824

commit v4 on v3

--- a/solution.py
+++ b/solution.py
@@ -66,6 +66,15 @@
     def device_of(grp, slot):
         return (grp * 4 + slot % 4, orbital * 2 + slot // 4)
 
+    def far(i):
+        return 2 - i + 3 * (i // 2) - 2 * (i // 3)
+
+    def to_group(i):
+        return (mine // 4 + far(i // 4)) % 4 * 4 + (mine + far(i % 4)) % 4
+
+    def from_group(i):
+        return (mine // 4 + 4 - far(i // 4)) % 4 * 4 + (mine + 4 - far(i % 4)) % 4
+
     barrier = pltpu.get_barrier_semaphore()
 
     def tell(semaphore, grp, slot):
@@ -134,25 +143,35 @@
 
     pl.semaphore_wait(plane_in, 7)
 
-    def send1(t, carry):
-        grp = (mine + t) % 16
+    def pack1(t):
+        grp = to_group(t)
         for slot in range(8):
             q = (slot // 4) * 64 + grp * 4 + slot % 4
             start = pl.multiple_of(q * PAD, 8)
             value = pages[pl.ds(start, hk), :].astype(BF)
             packed1[grp, slot] = value.reshape(hk // 2, 2, width)
-        for slot in range(8):
-            @pl.when((t != 0) | (slot != place))
-            def _():
-                pltpu.make_async_remote_copy(
-                    src_ref=packed1.at[grp, slot], dst_ref=landed1.at[mine, place],
-                    send_sem=ssem1, recv_sem=rsem1.at[t],
-                    device_id=device_of(grp, slot), device_id_type=MESH,
-                ).start()
-        return carry
-
-    lax.fori_loop(0, 16, send1, 0)
-    own1 = pltpu.make_async_copy(packed1.at[mine, place], landed1.at[mine, place], lsem)
+
+    def send(packed, landed, sent, came, t, s):
+        grp, slot = to_group(t), place ^ s
+        pltpu.make_async_remote_copy(
+            src_ref=packed.at[grp, slot], dst_ref=landed.at[mine, place],
+            send_sem=sent, recv_sem=came.at[t],
+            device_id=device_of(grp, slot), device_id_type=MESH,
+        ).start()
+
+    def send1(i, carry):
+        for u in range(1):
+            pack1(i * 1 + u)
+        for s in (6, 2, 7, 3, 4, 5, 1, 0):
+            for u in range(1):
+                send(packed1, landed1, ssem1, rsem1, i * 1 + u, s)
+        return carry
+
+    lax.fori_loop(0, 15, send1, 0)
+    pack1(15)
+    for s in (6, 2, 7, 3, 4, 5, 1):
+        send(packed1, landed1, ssem1, rsem1, 15, s)
+    own1 = pltpu.make_async_copy(packed1.at[mine, place], landed1.at[mine, place], rsem1.at[15])
     own1.start()
 
     for fetch in fetches[2:]:
@@ -200,20 +219,12 @@
 
     lax.fori_loop(0, 48, widen, 0)
     xbuf[...] = jnp.zeros_like(xbuf)
-    own1.wait()
 
     def arrive1(t, carry):
-        grp = (mine + 16 - t) % 16
-
-        @pl.when(t == 0)
-        def _():
-            ref = landed1.at[grp, pl.ds(0, 7)]
-            pltpu.make_async_copy(ref, ref, rsem1.at[t]).wait()
-
-        @pl.when(t != 0)
-        def _():
-            ref = landed1.at[grp]
-            pltpu.make_async_copy(ref, ref, rsem1.at[t]).wait()
+        grp = from_group(t)
+
+        ref = landed1.at[grp]
+        pltpu.make_async_copy(ref, ref, rsem1.at[t]).wait()
 
         for i in range(4):
             v0 = landed1[grp, i].reshape(hk, width).astype(F32)
@@ -277,8 +288,8 @@
 
     lax.fori_loop(0, 48 // together, distances, 0)
 
-    def send2(t, carry):
-        grp = (mine + t) % 16
+    def pack2(t):
+        grp = to_group(t)
         value = jnp.concatenate(
             [utab[pl.ds(grp * 3 + u, 48, stride=48), :] for u in range(3)], axis=0
         )
@@ -291,18 +302,20 @@
             second = jnp.where(low32, pltpu.roll(v0, 96, 1), v1)
             packed2[grp, i] = first[:hk].astype(BF).reshape(hk // 2, 2, width)
             packed2[grp, 4 + i] = second[:hk].astype(BF).reshape(hk // 2, 2, width)
-        for slot in range(8):
-            @pl.when((t != 0) | (slot != place))
-            def _():
-                pltpu.make_async_remote_copy(
-                    src_ref=packed2.at[grp, slot], dst_ref=landed2.at[mine, place],
-                    send_sem=ssem2, recv_sem=rsem2.at[t],
-                    device_id=device_of(grp, slot), device_id_type=MESH,
-                ).start()
-        return carry
-
-    lax.fori_loop(0, 16, send2, 0)
-    own2 = pltpu.make_async_copy(packed2.at[mine, place], landed2.at[mine, place], lsem)
+
+    def send2(i, carry):
+        for u in range(1):
+            pack2(i * 1 + u)
+        for s in (6, 2, 7, 3, 4, 5, 1, 0):
+            for u in range(1):
+                send(packed2, landed2, ssem2, rsem2, i * 1 + u, s)
+        return carry
+
+    lax.fori_loop(0, 15, send2, 0)
+    pack2(15)
+    for s in (6, 2, 7, 3, 4, 5, 1):
+        send(packed2, landed2, ssem2, rsem2, 15, s)
+    own2 = pltpu.make_async_copy(packed2.at[mine, place], landed2.at[mine, place], rsem2.at[15])
     own2.start()
 
     swap(0).wait()
@@ -319,20 +332,12 @@
         return carry
 
     lax.fori_loop(0, count_k, build, 0)
-    own2.wait()
 
     def arrive2(t, carry):
-        grp = (mine + 16 - t) % 16
-
-        @pl.when(t == 0)
-        def _():
-            ref = landed2.at[grp, pl.ds(0, 7)]
-            pltpu.make_async_copy(ref, ref, rsem2.at[t]).wait()
-
-        @pl.when(t != 0)
-        def _():
-            ref = landed2.at[grp]
-            pltpu.make_async_copy(ref, ref, rsem2.at[t]).wait()
+        grp = from_group(t)
+
+        ref = landed2.at[grp]
+        pltpu.make_async_copy(ref, ref, rsem2.at[t]).wait()
 
         for slot in range(8):
             value = landed2[grp, slot].reshape(hk, width).astype(F32)

time: 55.9 us -> 55.2 us (0.987)
  no operation moved by 1% of the time
where the time goes in v4:
time: 55.2 us; the launch traced here: 55.1 us
  Pallas kernels  53 us (96%)
  local copies, waits for them, and re-layouts  1.43 us (3%)
  between operations  0.64 us (1%)
    pallas_call x1, Pallas kernels, on_device(): pl.pallas_call(kernel, out_shape=(out, out), in_specs=[pl.BlockSpec(memor...  53 us
    unnamed x2, local copies, waits for them, and re-layouts  1.43 us

profile of v4, /device:TPU:1, one launch (start us, length us, event | category | flops | bytes accessed | tf_op | source)
XLA Modules:
  0.0 55.1 jit_solution(11948820812792990947)
XLA Ops:
  0.6 53.0 %shard_map.113 = (bf16[36,32,128]{2,1,0:T(8,128)(2,1)S(1)}, bf16[36,32,128]{2,1,0:T(8,128)(2,1)S(1)}) custom-call(bf16[36,32,128]{2,1,0:T(8,128)(2,1)} %green_in.1, bf16[2304,256]{1,0:T(8,128)(2,1)} %bitcast.3, f32[2,36]{1,0:T(2,128)} %bitcast.5, f32[64,128]{1,0:T(8,128)} %basis_in.1, f32[64,128]{1,0:T(8,128)} %bitcast.4, f32[64,64]{1,0:T(8,128)} %memk_in.1, ...), custom_call_target="tpu_custom_call" | custom-call | tf_op jit(solution)/shard_map/pallas_call | solution.py:395
  53.7 0.7 %copy.14 = bf16[36,32,128]{2,1,0:T(8,128)(2,1)} copy(bf16[36,32,128]{2,1,0:T(8,128)(2,1)S(1)} %get-tuple-element.2) | data formatting | bytes 589824
  54.4 0.7 %copy.15 = bf16[36,32,128]{2,1,0:T(8,128)(2,1)} copy(bf16[36,32,128]{2,1,0:T(8,128)(2,1)S(1)} %get-tuple-element.3) | data formatting | bytes 589824

commit v5 on v4

--- a/solution.py
+++ b/solution.py
@@ -51,7 +51,7 @@
 
 def kernel(
     green_in, screen_in, energy_in, basis_in, proj_in, memk_in, xf_in, xi_in, yf_in, yi_in,
-    sigma_ref, next_ref,
+    both_ref,
     green_ref, w_raw, energy_ref, basis_ref, proj_ref, memk_ref, xf_ref, xi_ref, yf_ref, yi_ref,
     fsem, plane_in, wre_full, wim_full, pages, packed1, landed1, packed2, landed2, ytab, utab, xbuf,
     tb, pb, pq, kb, pt, partner, gmat, amat, skm,
@@ -361,16 +361,17 @@
         at = pl.multiple_of(i * 1152, 32)
         value = amat[pl.ds(at, 1152), :]
         sigma = (dot(value, pq[0:256, :]) + dot(value, pq[256:512, :])).astype(BF)
-        sigma_ref[pl.ds(i * 36, 36)] = sigma.reshape(36, rows_m, width)
+        both_ref[:, :, 0:128] = sigma.reshape(36, rows_m, width).astype(F32)
         skm[pl.ds(at, 1152), :] = dot(jnp.concatenate([sigma, sigma], axis=1), kb[...]).astype(BF)
-        for u in range(36):
-            k = i * 36 + u
-            row = pl.multiple_of(i * 1152 + u * 32, 32)
-            memory = dot(skm[pl.ds(row, rows_m), :], gmat[k])
-            turned = gmat[k, pl.ds(mine_at, rows_m), :].astype(F32)
-            own = green_ref[k].astype(F32)
-            energy = energy_ref[orbital, k]
-            next_ref[k] = (own + STEP_SIZE * (energy * turned + memory)).astype(BF)
+        for u in range(0, 36, 2):
+            pair = dot(
+                skm[u * 32:u * 32 + 64, :], jnp.concatenate([gmat[u], gmat[u + 1]], axis=1)
+            )
+            for k, memory in ((u, pair[:rows_m, :128]), (u + 1, pair[rows_m:, 128:])):
+                turned = gmat[k, pl.ds(mine_at, rows_m), :].astype(F32)
+                own = green_ref[k].astype(F32)
+                energy = energy_ref[orbital, k]
+                both_ref[k, :, 128:256] = own + STEP_SIZE * (energy * turned + memory)
         return carry
 
     lax.fori_loop(0, count_k // 36, coeffs, 0)
@@ -391,12 +392,12 @@
     vmem = pl.BlockSpec(memory_space=pltpu.VMEM)
     dma = pltpu.SemaphoreType.DMA
     message = (16, 8, 9, 2, 128)
-    out = pltpu.VMEM(green_coeff.shape, BF)
-    return pl.pallas_call(
+    out = pltpu.VMEM((36, 32, 256), F32)
+    both = pl.pallas_call(
         kernel,
-        out_shape=(out, out),
+        out_shape=out,
         in_specs=[pl.BlockSpec(memory_space=pl.ANY)] * 10,
-        out_specs=(vmem, vmem),
+        out_specs=vmem,
         scratch_shapes=[
             pltpu.VMEM(green_coeff.shape, BF),
             pltpu.VMEM((total_k, 256), BF),
@@ -440,6 +441,7 @@
         memory_kernel,
         *tables,
     )
+    return both[:, :, :128].astype(BF), both[:, :, 128:].astype(BF)
 
 
 def solution(mesh):

time: 55.2 us -> 54.6 us (0.989)
    unnamed x2 -> x0, local copies, waits for them, and re-layouts: 1.43 us -> none
    slice x0 -> x1, local copies, waits for them, and re-layouts: none -> 0.91 us  [on_device(): return (both[:, :, :128].astype(BF), both[:, :, 128:].astype(BF))]
where the time goes in v5:
time: 54.6 us; the launch traced here: 54.5 us
  Pallas kernels  52.9 us (97%)
  local copies, waits for them, and re-layouts  0.91 us (2%)
  between operations  0.65 us (1%)
    pallas_call x1, Pallas kernels, on_device(): pl.pallas_call(kernel, out_shape=out, in_specs=[pl.BlockSpec(memory_space...  52.9 us

profile of v5, /device:TPU:1, one launch (start us, length us, event | category | flops | bytes accessed | tf_op | source)
XLA Modules:
  0.0 54.5 jit_solution(18069720946620194725)
XLA Ops:
  0.6 52.9 %shard_map.113 = f32[36,32,256]{2,1,0:T(8,128)S(1)} custom-call(bf16[36,32,128]{2,1,0:T(8,128)(2,1)} %green_in.1, bf16[2304,256]{1,0:T(8,128)(2,1)} %bitcast.3, f32[2,36]{1,0:T(2,128)} %bitcast.5, f32[64,128]{1,0:T(8,128)} %basis_in.1, f32[64,128]{1,0:T(8,128)} %bitcast.4, f32[64,64]{1,0:T(8,128)} %memk_in.1, bf16[288,144]{1,0:T(8,128)(2,1)} %constant.8.clone.xf_in, ...), custom_call_target="tpu_custom_call" | custom-call | tf_op jit(solution)/shard_map/pallas_call | solution.py:396
  53.5 0.1 convert.4
  53.6 0.9 %fusion = (bf16[36,32,128]{2,1,0:T(8,128)(2,1)}, bf16[36,32,128]{2,1,0:T(8,128)(2,1)}) fusion(bf16[36,32,256]{2,1,0:T(8,128)(2,1)S(1)} %convert.4), kind=kLoop, calls=%fused_computation | loop fusion | bytes 1179648 | tf_op jit(solution)/shard_map/slice | solution.py:444

commit v6 on v5

--- a/solution.py
+++ b/solution.py
@@ -408,15 +408,15 @@
             *[pltpu.VMEM(t.shape, BF) for t in tables],
             dma((10,)),
             pltpu.SemaphoreType.REGULAR,
-            pltpu.VMEM((total_k, 128), F32),
-            pltpu.VMEM((total_k, 128), F32),
-            pltpu.VMEM((128 * PAD, 128), F32),
+            pltpu.VMEM((total_k + 48, 128), F32),
+            pltpu.VMEM((total_k + 48, 128), F32),
+            pltpu.VMEM((129 * PAD, 128), F32),
             pltpu.VMEM(message, BF),
             pltpu.VMEM(message, BF),
             pltpu.VMEM(message, BF),
             pltpu.VMEM(message, BF),
-            pltpu.VMEM((total_k, 128), F32),
-            pltpu.VMEM((total_k, 128), F32),
+            pltpu.VMEM((total_k + 48, 128), F32),
+            pltpu.VMEM((total_k + 48, 128), F32),
             pltpu.VMEM((8 * PAD, 128), F32),
             pltpu.VMEM((256, 256), BF),
             pltpu.VMEM((512, 128), BF),

time: 54.6 us -> 54.6 us (level)
  no operation moved by 1% of the time
where the time goes in v6:
time: 54.6 us
  Pallas kernels  52.9 us (97%)
  local copies, waits for them, and re-layouts  0.91 us (2%)
  between operations  0.65 us (1%)
    pallas_call x1, Pallas kernels, on_device(): pl.pallas_call(kernel, out_shape=out, in_specs=[pl.BlockSpec(memory_space...  52.9 us

profile of v6, /device:TPU:1, one launch (start us, length us, event | category | flops | bytes accessed | tf_op | source)
XLA Modules:
  0.0 54.6 jit_solution(4530105072052535192)
XLA Ops:
  0.6 52.9 %shard_map.113 = f32[36,32,256]{2,1,0:T(8,128)S(1)} custom-call(bf16[36,32,128]{2,1,0:T(8,128)(2,1)} %green_in.1, bf16[2304,256]{1,0:T(8,128)(2,1)} %bitcast.3, f32[2,36]{1,0:T(2,128)} %bitcast.5, f32[64,128]{1,0:T(8,128)} %basis_in.1, f32[64,128]{1,0:T(8,128)} %bitcast.4, f32[64,64]{1,0:T(8,128)} %memk_in.1, bf16[288,144]{1,0:T(8,128)(2,1)} %constant.8.clone.xf_in, ...), custom_call_target="tpu_custom_call" | custom-call | tf_op jit(solution)/shard_map/pallas_call | solution.py:396
  53.5 0.1 convert.4
  53.6 0.9 %fusion = (bf16[36,32,128]{2,1,0:T(8,128)(2,1)}, bf16[36,32,128]{2,1,0:T(8,128)(2,1)}) fusion(bf16[36,32,256]{2,1,0:T(8,128)(2,1)S(1)} %convert.4), kind=kLoop, calls=%fused_computation | loop fusion | bytes 1179648 | tf_op jit(solution)/shard_map/slice | solution.py:444
